TPU v7x, 128 devices: a whole 4x4x4 slice. The times are simulated.
128 devices in a mesh: mom: 8 (over y, core), pair: 16 (over x, z).
Axes of the slice: x: 4, y: 4, z: 4, core: 2. Of those that a mesh axis runs over, the one named last changes fastest.
Arguments:
- blocks: bfloat16 [8, 16, 1024, 1024], P('mom', None, 'pair'), may hold values from -1.078125 to 1.078125
- left_ids: int32 [8, 48], P('mom', 'pair'), may hold values from 0 to 15
- right_ids: int32 [8, 48], P('mom', 'pair'), may hold values from 0 to 15
- slice_ids: int32 [8, 48], P('mom', 'pair'), may hold values from 0 to 1
- weight_ids: int32 [8, 48], P('mom', 'pair'), may hold values from 0 to 7
- counts: int32 [8, 16], P('mom', 'pair'), may hold values from 1 to 3, 32 in all within a row
- subduction: float32 [8], replicated, may hold values from -1 to 1
Outputs:
- operator: float32 [8, 1024, 2, 1024], P('mom', 'pair')
Inputs may be any that keep to these rules, and one draw needn't show every extreme that they name: Each row of counts sums to exactly 32.
All inputs are finite; a program needn't handle non-finite values. No bound on the sum of `counts` on one device may be relied on, other than what follows from the above.
Results may differ from a plain program's by a relative error of at most 0.0029.
Values may be sent and summed in bfloat16 or wider, within the bound.
A program may use at most 128 MiB of HBM per device.

v0:
```python
import jax
import jax.numpy as jnp
from jax import lax
from jax.sharding import PartitionSpec as P

PAIR_DEV = 3
SLICES = 2


def partner_2(shard, axis, apart):
    return lax.ppermute(shard, axis, [(i, i ^ 1 << apart) for i in range(lax.axis_size(axis))])


def mixing_table(lefts, rights, slices, weights, allowed, subduction, families):
    total_slots = lefts.shape[0]
    slot = jnp.arange(total_slots, dtype=jnp.int32)
    list_of = slot // PAIR_DEV
    lists = jnp.arange(allowed.shape[0], dtype=jnp.int32)
    limit = jnp.sum(jnp.where(list_of[:, None] == lists[None, :], allowed[None, :], 0), axis=1)
    live = slot % PAIR_DEV < limit
    table_ids = jnp.arange(subduction.shape[0], dtype=jnp.int32)
    looked = jnp.sum(
        jnp.where(weights[:, None] == table_ids[None, :], subduction[None, :], 0.0), axis=1
    )
    select = (slices[:, None] == jnp.arange(SLICES, dtype=jnp.int32)[None, :]).astype(jnp.float32)
    scales = jnp.where(live, looked, 0.0)[:, None] * select
    fam_ids = jnp.arange(families, dtype=jnp.int32)
    right_hot = (rights[:, None] == fam_ids[None, :]).astype(jnp.float32)
    left_hot = (lefts[:, None] == fam_ids[None, :]).astype(jnp.float32)
    return jnp.einsum("kt,kb,ka->tba", scales, right_hot, left_hot, precision=lax.Precision.HIGHEST)


def combine_left(mixing, panels):
    families = panels.shape[0]
    flat = panels.astype(jnp.float32).reshape(families, -1)
    mixed = jnp.dot(
        mixing.reshape(SLICES * families, families), flat, precision=lax.Precision.HIGHEST
    )
    return mixed.astype(jnp.bfloat16).reshape((SLICES, families) + panels.shape[1:])


def body(blocks, left_ids, right_ids, slice_ids, weight_ids, counts, subduction):
    gathered = (
        lax.all_gather(left_ids, "pair", axis=1, tiled=True),
        lax.all_gather(right_ids, "pair", axis=1, tiled=True),
        lax.all_gather(slice_ids, "pair", axis=1, tiled=True),
        lax.all_gather(weight_ids, "pair", axis=1, tiled=True),
        lax.all_gather(counts, "pair", axis=1, tiled=True),
    )
    own = blocks[0]
    families = own.shape[0]
    mixing = mixing_table(
        gathered[0][0],
        gathered[1][0],
        gathered[2][0],
        gathered[3][0],
        gathered[4][0],
        subduction,
        families,
    )
    partner = partner_2(own, "mom", 0)
    combined = combine_left(mixing, own)
    result = jnp.einsum(
        "tbij,bjl->itl",
        combined,
        lax.all_gather(partner, "pair", axis=1, tiled=True),
        preferred_element_type=jnp.float32,
    )
    return result.reshape((1,) + result.shape)


def solution(mesh):
    return jax.shard_map(
        body,
        mesh=mesh,
        in_specs=(
            P("mom", None, "pair", None),
            P("mom", "pair"),
            P("mom", "pair"),
            P("mom", "pair"),
            P("mom", "pair"),
            P("mom", "pair"),
            P(),
        ),
        out_specs=P("mom", "pair", None, None),
        check_vma=False,
    )
```

profile of v0, /device:TPU:1, one launch (start us, length us, event | category | flops | bytes accessed | tf_op | source)
XLA Modules:
  0.0 235.2 jit_solution(4597328169797305027)
XLA Ops:
  6.5 0.0 copy-start.5
  6.6 0.0 all-gather.2.cloned.1.call-start
  6.6 1.5 collective-permute-start
  8.1 4.0 %collective-permute-done = bf16[16,64,1024]{2,1,0:T(8,128)(2,1)S(1)} collective-permute-done((bf16[16,64,1024]{2,1,0:T(8,128)(2,1)}, bf16[16,64,1024]{2,1,0:T(8,128)(2,1)S(1)}, u32[]{:S(2)}, u32[]{:S(2)}) %collective-permute-start) | collective-permute-done | bytes 2097184 | tf_op jit(solution)/shard_map/ppermute | solution.py:11
  12.1 1.3 copy-done
  13.4 0.0 all-gather.2.cloned.1.call-update
  14.1 2.7 %copy.11 = bf16[2,8,64,1024]{3,1,2,0:T(8,128)(2,1)S(1)} copy(bf16[2,8,64,1024]{3,2,1,0:T(8,128)(2,1)} %bitcast.49) | data formatting | bytes 4194304
  16.8 0.0 copy-done.6
  16.9 0.6 dynamic-slice
  18.1 0.7 bitcast_dynamic-update-slice_fusion.2
  18.8 0.0 copy-done.1
  18.8 0.1 bitcast_dynamic-update-slice_fusion.4
  18.9 0.1 bitcast_dynamic-update-slice_fusion.1
  19.0 0.1 bitcast_dynamic-update-slice_fusion.3
  19.1 0.1 bitcast_dynamic-update-slice_fusion
  19.2 13.6 %all-reduce.5 = (s32[48]{0:T(128)S(1)}, s32[48]{0:T(128)S(1)}, s32[16]{0:T(128)S(1)}, s32[48]{0:T(128)S(1)}, s32[48]{0:T(128)S(1)}) all-reduce(s32[48]{0:T(128)S(1)} %bitcast_dynamic-update-slice_fusion.3, s32[48]{0:T(128)S(1)} %bitcast_dynamic-update-slice_fusion.1, ...), channel_id=1, replica_groups=mesh['mom'=8,'pair'=16] {'pair'}, use_global_device_ids=true, to_apply=%add.1 | all-reduce | flops 208 | bytes 1664
  32.9 0.1 select_reduce_fusion.1
  32.9 0.1 select_reduce_fusion
  33.1 0.1 fusion.8
  33.2 3.6 %convolution_convert_fusion = bf16[32,65536]{1,0:T(8,128)(2,1)S(1)} fusion(f32[32,16]{1,0:T(8,128)S(1)} %bitcast.50, bf16[16,65536]{1,0:T(8,128)(2,1)S(1)} %bitcast.47), kind=kOutput, calls=%fused_computation | convolution fusion | flops 404750336 | bytes 6293504 | tf_op jit(solution)/shard_map/dot_general | solution.py:36
  36.8 4.4 %copy.12 = bf16[4,8,64,1024]{3,2,1,0:T(8,128)(2,1)} copy(bf16[4,8,64,1024]{3,1,2,0:T(8,128)(2,1)S(1)} %bitcast.46) | data formatting | bytes 8388608
  41.1 171.9 %all-gather.2.cloned.1.call-done = bf16[16,1024,1024]{2,1,0:T(8,128)(2,1)} async-done(((bf16[16,64,1024]{2,1,0:T(8,128)(2,1)}), bf16[16,1024,1024]{2,1,0:T(8,128)(2,1)}) %all-gather.2.cloned.1.call-update) | async-done | bytes 33554448 | tf_op jit(solution)/shard_map/all_gather | solution.py:66
  213.0 14.1 %fusion.3 = f32[1,64,2,1024]{3,1,2,0:T(8,128)S(1)} fusion(bf16[16,1024,1024]{2,1,0:T(8,128)(2,1)} %all-gather.2.cloned.1.call-done, bf16[2,16,64,1024]{3,2,1,0:T(8,128)(2,1)} %bitcast.45), kind=kOutput, calls=%fused_computation.4 | convolution fusion | flops 4294967296 | bytes 38273024 | tf_op jit(solution)/shard_map/tbij,bjl->itl/dot_general | solution.py:63
  227.1 1.2 copy.9
  (19 shorter events, 0.1 us)
Async XLA Ops:
  6.5 10.3 %copy-start.6 = (u32[128]{0:T(128)S(1)}, u32[128]{0:T(128)}, u32[]{:S(2)}) copy-start(u32[128]{0:T(128)} %constant.32) | copy-start | bytes 1540
  6.5 12.3 %copy-start.1 = (s32[1,3]{1,0:T(1,128)S(1)}, s32[1,3]{1,0:T(1,128)}, u32[]{:S(2)}) copy-start(s32[1,3]{1,0:T(1,128)} %param.9) | copy-start | bytes 40
  6.5 12.4 %copy-start.2 = (s32[1,3]{1,0:T(1,128)S(1)}, s32[1,3]{1,0:T(1,128)}, u32[]{:S(2)}) copy-start(s32[1,3]{1,0:T(1,128)} %param.11) | copy-start | bytes 40
  6.5 12.5 %copy-start.3 = (s32[1,3]{1,0:T(1,128)S(1)}, s32[1,3]{1,0:T(1,128)}, u32[]{:S(2)}) copy-start(s32[1,3]{1,0:T(1,128)} %param.10) | copy-start | bytes 40
  6.5 12.6 %copy-start.4 = (s32[1,3]{1,0:T(1,128)S(1)}, s32[1,3]{1,0:T(1,128)}, u32[]{:S(2)}) copy-start(s32[1,3]{1,0:T(1,128)} %param.8) | copy-start | bytes 40
  6.5 26.3 %copy-start.5 = (f32[8]{0:T(128)S(1)}, f32[8]{0:T(128)}, u32[]{:S(2)}) copy-start(f32[8]{0:T(128)} %param.13) | copy-start | bytes 100
  6.6 206.5 %all-gather.2.cloned.1.call-start = ((), (), s32[]{:S(2)}) async-start(), calls=%async_computation | async-start | bytes 35651584 | tf_op jit(solution)/shard_map/all_gather | solution.py:66
  6.6 5.5 %collective-permute-start = (bf16[16,64,1024]{2,1,0:T(8,128)(2,1)}, bf16[16,64,1024]{2,1,0:T(8,128)(2,1)S(1)}, u32[]{:S(2)}, u32[]{:S(2)}) collective-permute-start(bf16[16,64,1024]{2,1,0:T(8,128)(2,1)} %bitcast.48), channel_id=1, source_target_pairs={{0,16},{16,0},{32,48},{48,32},{64,80},{80,64},{96,112},{112,96},{1... | collective-permute-start | bytes 6291464 | tf_op jit(solution)/shard_map/ppermute | solution.py:11
  12.1 1.3 copy-start
Sparse Core Ops, SparseCore 0:
  13.6 199.4 all-gather.1
where the time goes:
time: 235 us
  waiting for transfers between devices  176 us (75%)
  matrix products  17.8 us (8%)
  between operations  14.8 us (6%)
  blocking collectives  13.6 us (6%)
  local copies, waits for them, and re-layouts  11.3 us (5%)
    all_gather x1, waiting for transfers between devices, body(): lax.all_gather(partner, 'pair', axis=1, tiled=True)  172 us
    dot_general x1, matrix products, body(): jnp.einsum('tbij,bjl->itl', combined, lax.all_gather(partner, 'pair', axi...  14.1 us
    unnamed x1, blocking collectives  13.6 us
    unnamed x27, local copies, waits for them, and re-layouts  10.1 us
  transfers between devices with their start and end apart: 2, of which 2 were waited for; matrix products, arithmetic and copies ran while one was open for 5% of the time, Pallas kernels for 0%

commit v1 on v0

--- a/solution.py
+++ b/solution.py
@@ -5,6 +5,27 @@
 
 PAIR_DEV = 3
 SLICES = 2
+
+
+def collect(x, axis, dim):
+    length, index, span = (lax.axis_size(axis), lax.axis_index(axis), x.shape[dim])
+    upward = [(i, (i + 1) % length) for i in range(length)]
+    backward = [(i, (i - 1) % length) for i in range(length)]
+    out = jnp.zeros((*x.shape[:dim], length * span, *x.shape[dim + 1 :]), x.dtype)
+    out = lax.dynamic_update_slice_in_dim(out, x, index * span, axis=dim)
+    from_left = from_right = x
+    half = length // 2
+    for step in range(1, half + 1):
+        from_left = lax.ppermute(from_left, axis, upward)
+        out = lax.dynamic_update_slice_in_dim(
+            out, from_left, (index - step) % length * span, axis=dim
+        )
+        if step < length - half:
+            from_right = lax.ppermute(from_right, axis, backward)
+            out = lax.dynamic_update_slice_in_dim(
+                out, from_right, (index + step) % length * span, axis=dim
+            )
+    return out
 
 
 def partner_2(shard, axis, apart):
@@ -61,10 +82,7 @@
     partner = partner_2(own, "mom", 0)
     combined = combine_left(mixing, own)
     result = jnp.einsum(
-        "tbij,bjl->itl",
-        combined,
-        lax.all_gather(partner, "pair", axis=1, tiled=True),
-        preferred_element_type=jnp.float32,
+        "tbij,bjl->itl", combined, collect(partner, "pair", 1), preferred_element_type=jnp.float32
     )
     return result.reshape((1,) + result.shape)
 

time: 235 us -> 442 us (1.88)
  the two profiles are of different devices: /device:TPU:1 before, /device:TPU:0 now
where the time goes in v1:
time: 442 us
  waiting for transfers between devices  272 us (62%)
  local copies, waits for them, and re-layouts  64.4 us (15%)
  blocking collectives  46.4 us (10%)
  starting transfers between devices  40.1 us (9%)
  matrix products  17 us (4%)
    ppermute x8, waiting for transfers between devices, collect(): from_left = lax.ppermute(from_left, axis, upward)  257 us
    unnamed x1, blocking collectives  46.4 us
    ppermute x7, starting transfers between devices, collect(): from_right = lax.ppermute(from_right, axis, backward)  38 us
    dynamic_update_slice x8, local copies, waits for them, and re-layouts, collect(): lax.dynamic_update_slice_in_dim(out, from_left, (index - step) % length *...  16.6 us
    broadcast_in_dim x1, local copies, waits for them, and re-layouts, collect(): jnp.zeros((*x.shape[:dim], length * span, *x.shape[dim + 1:]), x.dtype)  16.1 us
    unnamed x49, local copies, waits for them, and re-layouts  15.5 us
    dynamic_update_slice x7, local copies, waits for them, and re-layouts, collect(): lax.dynamic_update_slice_in_dim(out, from_right, (index + step) % length...  13.6 us
    dot_general x1, matrix products, body(): jnp.einsum('tbij,bjl->itl', combined, collect(partner, 'pair', 1), prefer...  13.3 us
  transfers between devices with their start and end apart: 16, of which 11 were waited for; matrix products, arithmetic and copies ran while one was open for 14% of the time, Pallas kernels for 0%

profile of v1, /device:TPU:0, one launch (start us, length us, event | category | flops | bytes accessed | tf_op | source)
XLA Modules:
  0.0 441.8 jit_solution(11896751669837824995)
XLA Ops:
  0.0 4.4 collective-permute-done
  6.4 4.3 collective-permute-start.2
  10.7 45.9 %collective-permute-done.1 = bf16[16,64,1024]{2,1,0:T(8,128)(2,1)S(1)} collective-permute-done((bf16[16,64,1024]{2,1,0:T(8,128)(2,1)S(1)}, bf16[16,64,1024]{2,1,0:T(8,128)(2,1)S(1)}, u32[]{:S(2)}, u32[]{:S(2)}) %collective-permute-start.1) | collective-permute-done | bytes 2097184 | tf_op jit(solution)/shard_map/ppermute | solution.py:19
  58.0 5.3 %collective-permute-start.4 = (bf16[16,64,1024]{2,1,0:T(8,128)(2,1)S(1)}, bf16[16,64,1024]{2,1,0:T(8,128)(2,1)S(1)}, u32[]{:S(2)}, u32[]{:S(2)}) collective-permute-start(bf16[16,64,1024]{2,1,0:T(8,128)(2,1)S(1)} %collective-permute-done.2), channel_id=1, source_target_pairs={{0,15},{1,0},{2,1},{3,2},{4,3},{5,4},{6,5},{7,6},{8,7},{9,8},{10,9... | collective-permute-start | bytes 6291464 | tf_op jit(solution)/shard_map/ppermute | solution.py:24
  63.3 43.8 %collective-permute-done.3 = bf16[16,64,1024]{2,1,0:T(8,128)(2,1)S(1)} collective-permute-done((bf16[16,64,1024]{2,1,0:T(8,128)(2,1)S(1)}, bf16[16,64,1024]{2,1,0:T(8,128)(2,1)S(1)}, u32[]{:S(2)}, u32[]{:S(2)}) %collective-permute-start.3) | collective-permute-done | bytes 2097184 | tf_op jit(solution)/shard_map/ppermute | solution.py:19
  108.5 5.0 %collective-permute-start.6 = (bf16[16,64,1024]{2,1,0:T(8,128)(2,1)S(1)}, bf16[16,64,1024]{2,1,0:T(8,128)(2,1)S(1)}, u32[]{:S(2)}, u32[]{:S(2)}) collective-permute-start(bf16[16,64,1024]{2,1,0:T(8,128)(2,1)S(1)} %collective-permute-done.4), channel_id=1, source_target_pairs={{0,15},{1,0},{2,1},{3,2},{4,3},{5,4},{6,5},{7,6},{8,7},{9,8},{10,9... | collective-permute-start | bytes 6291464 | tf_op jit(solution)/shard_map/ppermute | solution.py:24
  113.5 43.2 %collective-permute-done.5 = bf16[16,64,1024]{2,1,0:T(8,128)(2,1)S(1)} collective-permute-done((bf16[16,64,1024]{2,1,0:T(8,128)(2,1)S(1)}, bf16[16,64,1024]{2,1,0:T(8,128)(2,1)S(1)}, u32[]{:S(2)}, u32[]{:S(2)}) %collective-permute-start.5) | collective-permute-done | bytes 2097184 | tf_op jit(solution)/shard_map/ppermute | solution.py:19
  157.0 5.8 %collective-permute-start.8 = (bf16[16,64,1024]{2,1,0:T(8,128)(2,1)S(1)}, bf16[16,64,1024]{2,1,0:T(8,128)(2,1)S(1)}, u32[]{:S(2)}, u32[]{:S(2)}) collective-permute-start(bf16[16,64,1024]{2,1,0:T(8,128)(2,1)S(1)} %collective-permute-done.6), channel_id=1, source_target_pairs={{0,15},{1,0},{2,1},{3,2},{4,3},{5,4},{6,5},{7,6},{8,7},{9,8},{10,9... | collective-permute-start | bytes 6291464 | tf_op jit(solution)/shard_map/ppermute | solution.py:24
  162.8 42.6 %collective-permute-done.7 = bf16[16,64,1024]{2,1,0:T(8,128)(2,1)S(1)} collective-permute-done((bf16[16,64,1024]{2,1,0:T(8,128)(2,1)S(1)}, bf16[16,64,1024]{2,1,0:T(8,128)(2,1)S(1)}, u32[]{:S(2)}, u32[]{:S(2)}) %collective-permute-start.7) | collective-permute-done | bytes 2097184 | tf_op jit(solution)/shard_map/ppermute | solution.py:19
  206.7 4.5 %collective-permute-start.10 = (bf16[16,64,1024]{2,1,0:T(8,128)(2,1)S(1)}, bf16[16,64,1024]{2,1,0:T(8,128)(2,1)}, u32[]{:S(2)}, u32[]{:S(2)}) collective-permute-start(bf16[16,64,1024]{2,1,0:T(8,128)(2,1)S(1)} %collective-permute-done.8), channel_id=1, source_target_pairs={{0,15},{1,0},{2,1},{3,2},{4,3},{5,4},{6,5},{7,6},{8,7},{9,8},{10,9... | collective-permute-start | bytes 6291464 | tf_op jit(solution)/shard_map/ppermute | solution.py:24
  211.1 42.1 %collective-permute-done.9 = bf16[16,64,1024]{2,1,0:T(8,128)(2,1)} collective-permute-done((bf16[16,64,1024]{2,1,0:T(8,128)(2,1)S(1)}, bf16[16,64,1024]{2,1,0:T(8,128)(2,1)}, u32[]{:S(2)}, u32[]{:S(2)}) %collective-permute-start.9) | collective-permute-done | bytes 2097184 | tf_op jit(solution)/shard_map/ppermute | solution.py:19
  256.6 5.4 %collective-permute-start.12 = (bf16[16,64,1024]{2,1,0:T(8,128)(2,1)}, bf16[16,64,1024]{2,1,0:T(8,128)(2,1)}, u32[]{:S(2)}, u32[]{:S(2)}) collective-permute-start(bf16[16,64,1024]{2,1,0:T(8,128)(2,1)} %collective-permute-done.10), channel_id=1, source_target_pairs={{0,15},{1,0},{2,1},{3,2},{4,3},{5,4},{6,5},{7,6},{8,7},{9,8},{10,9... | collective-permute-start | bytes 6291464 | tf_op jit(solution)/shard_map/ppermute | solution.py:24
  266.8 33.5 %collective-permute-done.11 = bf16[16,64,1024]{2,1,0:T(8,128)(2,1)} collective-permute-done((bf16[16,64,1024]{2,1,0:T(8,128)(2,1)}, bf16[16,64,1024]{2,1,0:T(8,128)(2,1)}, u32[]{:S(2)}, u32[]{:S(2)}) %collective-permute-start.11) | collective-permute-done | bytes 2097184 | tf_op jit(solution)/shard_map/ppermute | solution.py:19
  301.1 46.4 %all-reduce.5 = (s32[48]{0:T(128)S(1)}, s32[48]{0:T(128)S(1)}, s32[16]{0:T(128)S(1)}, s32[48]{0:T(128)S(1)}, s32[48]{0:T(128)S(1)}) all-reduce(s32[48]{0:T(128)S(1)} %bitcast_dynamic-update-slice_fusion.3, s32[48]{0:T(128)S(1)} %bitcast_dynamic-update-slice_fusion.1, ...), channel_id=1, replica_groups=mesh['mom'=8,'pair'=16] {'pair'}, use_global_device_ids=true, to_apply=%add.1 | all-reduce | flops 208 | bytes 1664
  348.5 3.6 convolution_convert_fusion
  352.1 4.4 copy.12
  356.5 16.1 %broadcast_in_dim.41 = bf16[16,1024,1024]{2,1,0:T(8,128)(2,1)} broadcast(bf16[]{:T(256)} %constant.106.clone.1), dimensions={} | broadcast | bytes 33554432 | tf_op jit(solution)/shard_map/broadcast_in_dim | solution.py:14
  374.1 7.7 %collective-permute-start.14 = (bf16[16,64,1024]{2,1,0:T(8,128)(2,1)}, bf16[16,64,1024]{2,1,0:T(8,128)(2,1)S(1)}, u32[]{:S(2)}, u32[]{:S(2)}) collective-permute-start(bf16[16,64,1024]{2,1,0:T(8,128)(2,1)} %collective-permute-done.12), channel_id=1, source_target_pairs={{0,15},{1,0},{2,1},{3,2},{4,3},{5,4},{6,5},{7,6},{8,7},{9,8},{10,9... | collective-permute-start | bytes 6291464 | tf_op jit(solution)/shard_map/ppermute | solution.py:24
  393.7 3.1 constant_dynamic-update-slice_fusion.6
  399.9 3.1 constant_dynamic-update-slice_fusion.4
  406.1 3.1 constant_dynamic-update-slice_fusion.2
  409.2 9.8 %collective-permute-done.14 = bf16[16,64,1024]{2,1,0:T(8,128)(2,1)S(1)} collective-permute-done((bf16[16,64,1024]{2,1,0:T(8,128)(2,1)}, bf16[16,64,1024]{2,1,0:T(8,128)(2,1)S(1)}, u32[]{:S(2)}, u32[]{:S(2)}) %collective-permute-start.14) | collective-permute-done | bytes 2097184 | tf_op jit(solution)/shard_map/ppermute | solution.py:24
  420.4 5.4 %collective-permute-done.15 = bf16[16,64,1024]{2,1,0:T(8,128)(2,1)S(1)} collective-permute-done((bf16[16,64,1024]{2,1,0:T(8,128)(2,1)}, bf16[16,64,1024]{2,1,0:T(8,128)(2,1)S(1)}, u32[]{:S(2)}, u32[]{:S(2)}) %collective-permute-start.15) | collective-permute-done | bytes 2097184 | tf_op jit(solution)/shard_map/ppermute | solution.py:19
  427.3 13.3 %fusion.3 = f32[1,64,2,1024]{3,1,2,0:T(8,128)S(1)} fusion(bf16[16,1024,1024]{2,1,0:T(8,128)(2,1)} %constant_dynamic-update-slice_fusion, bf16[2,16,64,1024]{3,2,1,0:T(8,128)(2,1)} %bitcast.45), kind=kOutput, calls=%fused_computation.4 | convolution fusion | flops 4294967296 | bytes 38273024 | tf_op jit(solution)/shard_map/tbij,bjl->itl/dot_general | solution.py:84
  (85 shorter events, 38.5 us)
Async XLA Ops:
  0.0 4.4 collective-permute-start
  4.4 52.3 %copy-start.10 = (bf16[16,64,1024]{2,1,0:T(8,128)(2,1)}, bf16[16,64,1024]{2,1,0:T(8,128)(2,1)S(1)}, u32[]{:S(2)}) copy-start(bf16[16,64,1024]{2,1,0:T(8,128)(2,1)S(1)} %collective-permute-done) | copy-start | bytes 6291460
  4.4 52.2 %collective-permute-start.1 = (bf16[16,64,1024]{2,1,0:T(8,128)(2,1)S(1)}, bf16[16,64,1024]{2,1,0:T(8,128)(2,1)S(1)}, u32[]{:S(2)}, u32[]{:S(2)}) collective-permute-start(bf16[16,64,1024]{2,1,0:T(8,128)(2,1)S(1)} %collective-permute-done), channel_id=1, source_target_pairs={{0,1},{1,2},{2,3},{3,4},{4,5},{5,6},{6,7},{7,8},{8,9},{9,10},{10,1... | collective-permute-start | bytes 6291464 | tf_op jit(solution)/shard_map/ppermute | solution.py:19
  6.4 50.3 %collective-permute-start.2 = (bf16[16,64,1024]{2,1,0:T(8,128)(2,1)S(1)}, bf16[16,64,1024]{2,1,0:T(8,128)(2,1)S(1)}, u32[]{:S(2)}, u32[]{:S(2)}) collective-permute-start(bf16[16,64,1024]{2,1,0:T(8,128)(2,1)S(1)} %collective-permute-done), channel_id=1, source_target_pairs={{0,15},{1,0},{2,1},{3,2},{4,3},{5,4},{6,5},{7,6},{8,7},{9,8},{10,9... | collective-permute-start | bytes 6291464 | tf_op jit(solution)/shard_map/ppermute | solution.py:24
  56.6 100.4 %copy-start.6 = (bf16[16,64,1024]{2,1,0:T(8,128)(2,1)}, bf16[16,64,1024]{2,1,0:T(8,128)(2,1)S(1)}, u32[]{:S(2)}) copy-start(bf16[16,64,1024]{2,1,0:T(8,128)(2,1)S(1)} %collective-permute-done.1) | copy-start | bytes 6291460
  56.6 50.5 %collective-permute-start.3 = (bf16[16,64,1024]{2,1,0:T(8,128)(2,1)S(1)}, bf16[16,64,1024]{2,1,0:T(8,128)(2,1)S(1)}, u32[]{:S(2)}, u32[]{:S(2)}) collective-permute-start(bf16[16,64,1024]{2,1,0:T(8,128)(2,1)S(1)} %collective-permute-done.1), channel_id=1, source_target_pairs={{0,1},{1,2},{2,3},{3,4},{4,5},{5,6},{6,7},{7,8},{8,9},{9,10},{10,1... | collective-permute-start | bytes 6291464 | tf_op jit(solution)/shard_map/ppermute | solution.py:19
  58.0 49.7 %collective-permute-start.4 = (bf16[16,64,1024]{2,1,0:T(8,128)(2,1)S(1)}, bf16[16,64,1024]{2,1,0:T(8,128)(2,1)S(1)}, u32[]{:S(2)}, u32[]{:S(2)}) collective-permute-start(bf16[16,64,1024]{2,1,0:T(8,128)(2,1)S(1)} %collective-permute-done.2), channel_id=1, source_target_pairs={{0,15},{1,0},{2,1},{3,2},{4,3},{5,4},{6,5},{7,6},{8,7},{9,8},{10,9... | collective-permute-start | bytes 6291464 | tf_op jit(solution)/shard_map/ppermute | solution.py:24
  107.1 49.6 %collective-permute-start.5 = (bf16[16,64,1024]{2,1,0:T(8,128)(2,1)S(1)}, bf16[16,64,1024]{2,1,0:T(8,128)(2,1)S(1)}, u32[]{:S(2)}, u32[]{:S(2)}) collective-permute-start(bf16[16,64,1024]{2,1,0:T(8,128)(2,1)S(1)} %collective-permute-done.3), channel_id=1, source_target_pairs={{0,1},{1,2},{2,3},{3,4},{4,5},{5,6},{6,7},{7,8},{8,9},{9,10},{10,1... | collective-permute-start | bytes 6291464 | tf_op jit(solution)/shard_map/ppermute | solution.py:19
  108.5 48.2 %copy-start.4 = (bf16[16,64,1024]{2,1,0:T(8,128)(2,1)}, bf16[16,64,1024]{2,1,0:T(8,128)(2,1)S(1)}, u32[]{:S(2)}) copy-start(bf16[16,64,1024]{2,1,0:T(8,128)(2,1)S(1)} %collective-permute-done.4) | copy-start | bytes 6291460
  108.5 48.5 %collective-permute-start.6 = (bf16[16,64,1024]{2,1,0:T(8,128)(2,1)S(1)}, bf16[16,64,1024]{2,1,0:T(8,128)(2,1)S(1)}, u32[]{:S(2)}, u32[]{:S(2)}) collective-permute-start(bf16[16,64,1024]{2,1,0:T(8,128)(2,1)S(1)} %collective-permute-done.4), channel_id=1, source_target_pairs={{0,15},{1,0},{2,1},{3,2},{4,3},{5,4},{6,5},{7,6},{8,7},{9,8},{10,9... | collective-permute-start | bytes 6291464 | tf_op jit(solution)/shard_map/ppermute | solution.py:24
  156.7 48.7 %collective-permute-start.7 = (bf16[16,64,1024]{2,1,0:T(8,128)(2,1)S(1)}, bf16[16,64,1024]{2,1,0:T(8,128)(2,1)S(1)}, u32[]{:S(2)}, u32[]{:S(2)}) collective-permute-start(bf16[16,64,1024]{2,1,0:T(8,128)(2,1)S(1)} %collective-permute-done.5), channel_id=1, source_target_pairs={{0,1},{1,2},{2,3},{3,4},{4,5},{5,6},{6,7},{7,8},{8,9},{9,10},{10,1... | collective-permute-start | bytes 6291464 | tf_op jit(solution)/shard_map/ppermute | solution.py:19
  157.0 48.4 %copy-start.12 = (bf16[16,64,1024]{2,1,0:T(8,128)(2,1)}, bf16[16,64,1024]{2,1,0:T(8,128)(2,1)S(1)}, u32[]{:S(2)}) copy-start(bf16[16,64,1024]{2,1,0:T(8,128)(2,1)S(1)} %collective-permute-done.6) | copy-start | bytes 6291460
  157.0 48.4 %collective-permute-start.8 = (bf16[16,64,1024]{2,1,0:T(8,128)(2,1)S(1)}, bf16[16,64,1024]{2,1,0:T(8,128)(2,1)S(1)}, u32[]{:S(2)}, u32[]{:S(2)}) collective-permute-start(bf16[16,64,1024]{2,1,0:T(8,128)(2,1)S(1)} %collective-permute-done.6), channel_id=1, source_target_pairs={{0,15},{1,0},{2,1},{3,2},{4,3},{5,4},{6,5},{7,6},{8,7},{9,8},{10,9... | collective-permute-start | bytes 6291464 | tf_op jit(solution)/shard_map/ppermute | solution.py:24
  205.4 47.8 %collective-permute-start.9 = (bf16[16,64,1024]{2,1,0:T(8,128)(2,1)S(1)}, bf16[16,64,1024]{2,1,0:T(8,128)(2,1)}, u32[]{:S(2)}, u32[]{:S(2)}) collective-permute-start(bf16[16,64,1024]{2,1,0:T(8,128)(2,1)S(1)} %collective-permute-done.7), channel_id=1, source_target_pairs={{0,1},{1,2},{2,3},{3,4},{4,5},{5,6},{6,7},{7,8},{8,9},{9,10},{10,1... | collective-permute-start | bytes 6291464 | tf_op jit(solution)/shard_map/ppermute | solution.py:19
  206.7 56.7 %copy-start.16 = (bf16[16,64,1024]{2,1,0:T(8,128)(2,1)}, bf16[16,64,1024]{2,1,0:T(8,128)(2,1)S(1)}, u32[]{:S(2)}) copy-start(bf16[16,64,1024]{2,1,0:T(8,128)(2,1)S(1)} %collective-permute-done.8) | copy-start | bytes 6291460
  206.7 49.9 %collective-permute-start.10 = (bf16[16,64,1024]{2,1,0:T(8,128)(2,1)S(1)}, bf16[16,64,1024]{2,1,0:T(8,128)(2,1)}, u32[]{:S(2)}, u32[]{:S(2)}) collective-permute-start(bf16[16,64,1024]{2,1,0:T(8,128)(2,1)S(1)} %collective-permute-done.8), channel_id=1, source_target_pairs={{0,15},{1,0},{2,1},{3,2},{4,3},{5,4},{6,5},{7,6},{8,7},{9,8},{10,9... | collective-permute-start | bytes 6291464 | tf_op jit(solution)/shard_map/ppermute | solution.py:24
  253.2 47.1 %collective-permute-start.11 = (bf16[16,64,1024]{2,1,0:T(8,128)(2,1)}, bf16[16,64,1024]{2,1,0:T(8,128)(2,1)}, u32[]{:S(2)}, u32[]{:S(2)}) collective-permute-start(bf16[16,64,1024]{2,1,0:T(8,128)(2,1)} %collective-permute-done.9), channel_id=1, source_target_pairs={{0,1},{1,2},{2,3},{3,4},{4,5},{5,6},{6,7},{7,8},{8,9},{9,10},{10,1... | collective-permute-start | bytes 6291464 | tf_op jit(solution)/shard_map/ppermute | solution.py:19
  256.6 117.5 %collective-permute-start.12 = (bf16[16,64,1024]{2,1,0:T(8,128)(2,1)}, bf16[16,64,1024]{2,1,0:T(8,128)(2,1)}, u32[]{:S(2)}, u32[]{:S(2)}) collective-permute-start(bf16[16,64,1024]{2,1,0:T(8,128)(2,1)} %collective-permute-done.10), channel_id=1, source_target_pairs={{0,15},{1,0},{2,1},{3,2},{4,3},{5,4},{6,5},{7,6},{8,7},{9,8},{10,9... | collective-permute-start | bytes 6291464 | tf_op jit(solution)/shard_map/ppermute | solution.py:24
  300.3 82.9 %collective-permute-start.13 = (bf16[16,64,1024]{2,1,0:T(8,128)(2,1)}, bf16[16,64,1024]{2,1,0:T(8,128)(2,1)}, u32[]{:S(2)}, u32[]{:S(2)}) collective-permute-start(bf16[16,64,1024]{2,1,0:T(8,128)(2,1)} %collective-permute-done.11), channel_id=1, source_target_pairs={{0,1},{1,2},{2,3},{3,4},{4,5},{5,6},{6,7},{7,8},{8,9},{9,10},{10,1... | collective-permute-start | bytes 6291464 | tf_op jit(solution)/shard_map/ppermute | solution.py:19
  356.5 32.7 %copy-start.13 = (bf16[16,64,1024]{2,1,0:T(8,128)(2,1)S(1)}, bf16[16,64,1024]{2,1,0:T(8,128)(2,1)}, u32[]{:S(2)}) copy-start(bf16[16,64,1024]{2,1,0:T(8,128)(2,1)} %copy-done.12) | copy-start | bytes 6291460
  356.5 34.2 %copy-start.15 = (bf16[16,64,1024]{2,1,0:T(8,128)(2,1)S(1)}, bf16[16,64,1024]{2,1,0:T(8,128)(2,1)}, u32[]{:S(2)}) copy-start(bf16[16,64,1024]{2,1,0:T(8,128)(2,1)} %copy-done.14) | copy-start | bytes 6291460
  356.5 35.7 %copy-start.17 = (bf16[16,64,1024]{2,1,0:T(8,128)(2,1)S(1)}, bf16[16,64,1024]{2,1,0:T(8,128)(2,1)}, u32[]{:S(2)}) copy-start(bf16[16,64,1024]{2,1,0:T(8,128)(2,1)} %copy-done.16) | copy-start | bytes 6291460
  374.1 44.9 %collective-permute-start.14 = (bf16[16,64,1024]{2,1,0:T(8,128)(2,1)}, bf16[16,64,1024]{2,1,0:T(8,128)(2,1)S(1)}, u32[]{:S(2)}, u32[]{:S(2)}) collective-permute-start(bf16[16,64,1024]{2,1,0:T(8,128)(2,1)} %collective-permute-done.12), channel_id=1, source_target_pairs={{0,15},{1,0},{2,1},{3,2},{4,3},{5,4},{6,5},{7,6},{8,7},{9,8},{10,9... | collective-permute-start | bytes 6291464 | tf_op jit(solution)/shard_map/ppermute | solution.py:24
  383.3 42.6 %collective-permute-start.15 = (bf16[16,64,1024]{2,1,0:T(8,128)(2,1)}, bf16[16,64,1024]{2,1,0:T(8,128)(2,1)S(1)}, u32[]{:S(2)}, u32[]{:S(2)}) collective-permute-start(bf16[16,64,1024]{2,1,0:T(8,128)(2,1)} %collective-permute-done.13), channel_id=1, source_target_pairs={{0,1},{1,2},{2,3},{3,4},{4,5},{5,6},{6,7},{7,8},{8,9},{9,10},{10,1... | collective-permute-start | bytes 6291464 | tf_op jit(solution)/shard_map/ppermute | solution.py:19
  (10 other events, 172.2 us)
